TPU v7x, 512 devices: a whole 4x4x16 slice. The times are simulated.
512 devices in a mesh: dp: 4 (over x), ctx: 16 (over z), tp: 8 (over y, core).
Axes of the slice: x: 4, y: 4, z: 16, core: 2. Of those that a mesh axis runs over, the one named last changes fastest.
Arguments:
- inputs: bfloat16 [4, 4096, 8192], P('dp', 'ctx', 'tp'), may hold values from -6 to 6
- cotangent: bfloat16 [4, 4096, 8192], P('dp', 'ctx', 'tp'), may hold values from -6 to 6
- residues: float32 [512, 16], P('tp'), may hold values from -3 to 3
- decay_rates: float32 [512, 16], P('tp'), may hold values from 4.8828125e-05 to 0.0333333333
- skip_gain: float32 [8192], P('tp'), may hold values from -1 to 1
Outputs:
- outputs: bfloat16 [4, 4096, 8192], P('dp', 'ctx', 'tp')
- grad_inputs: bfloat16 [4, 4096, 8192], P('dp', 'ctx', 'tp')
- grad_residues: float32 [512, 16], P('tp')
- grad_skip: float32 [8192], P('tp')
All inputs are finite; a program needn't handle non-finite values.
Results may differ from a plain program's by a relative error of at most 0.0014.
Values sent between devices are 32-bit elements; how exact they have to be, the bound alone decides.
A program may use at most 64 MiB of HBM per device.

v0:
```python
import math
import jax
import jax.numpy as jnp
from jax import lax
from jax.sharding import PartitionSpec as P

highest = lax.Precision.HIGHEST


def passed_along(value, axis, by):
    length = lax.axis_size(axis)
    pairs = [(i, i + by) for i in range(length) if 0 <= i + by < length]
    return lax.ppermute(value, axis, pairs)


def shards(inputs, cotangent, residues, decay_rates, skip_gain):
    local_batch, block_rows, channels = inputs.shape
    group_count, mode_count = residues.shape
    group_width = channels // group_count
    sub_rows = math.gcd(256, block_rows)
    sub_count = block_rows // sub_rows
    weight = jnp.sqrt(1.0 - jnp.exp(-2.0 * decay_rates))
    coefficient = residues * weight
    positions = jnp.arange(sub_rows, dtype=jnp.float32)
    center = (sub_rows - 1) / 2.0
    rate_cube = decay_rates[:, :, None]
    decay_down = jnp.exp(-rate_cube * (positions - center))
    decay_up = jnp.exp(rate_cube * (positions - center))
    from_start = jnp.exp(-rate_cube * positions)
    to_end = jnp.exp(-rate_cube * (sub_rows - 1.0 - positions))
    five_shape = (local_batch, sub_count, sub_rows, group_count, group_width)
    state_shape = (local_batch, mode_count, channels)
    state_split = (local_batch, mode_count, group_count, group_width)
    inputs_wide = inputs.astype(jnp.float32).reshape(five_shape)
    cotangent_wide = cotangent.astype(jnp.float32).reshape(five_shape)
    sub_ends = jnp.einsum("gmt,bktgc->kbmgc", to_end, inputs_wide, precision=highest)
    sub_starts = jnp.einsum("gmt,bktgc->kbmgc", from_start, cotangent_wide, precision=highest)
    device_end = sub_ends[0]
    device_start = sub_starts[sub_count - 1]
    end_states = device_end.reshape(state_shape)
    start_states = device_start.reshape(state_shape)
    channel_rates = jnp.repeat(decay_rates.T, group_width, axis=1) * float(block_rows)
    passing = jnp.exp(-channel_rates)

    def relay_turn(turn, carried):
        incoming_x, incoming_d = carried
        sent_x = incoming_x * passing + end_states
        sent_d = incoming_d * passing + start_states
        return (passed_along(sent_x, "ctx", 1), passed_along(sent_d, "ctx", -1))

    empty_states = jnp.zeros_like(end_states)
    state_before, state_after = lax.fori_loop(
        0, lax.axis_size("ctx") - 1, relay_turn, (empty_states, empty_states)
    )
    block_count = math.gcd(group_count, 16)
    per_block = group_count // block_count
    causal_mask = positions[:, None] >= positions[None, :]

    def by_groups(array):
        return array.reshape((block_count, per_block) + array.shape[1:])

    def data_blocks(array):
        return array.reshape(
            local_batch, sub_count, sub_rows, block_count, per_block, group_width
        ).transpose(3, 0, 1, 2, 4, 5)

    def local_block(pieces):
        coef_piece, down_piece, up_piece, weight_piece, wide_x, wide_d, half_x, half_d = pieces
        kernel = jnp.where(
            causal_mask,
            jnp.einsum("gm,gmt,gms->gts", coef_piece, down_piece, up_piece, precision=highest),
            0.0,
        )
        local_out = jnp.einsum("gts,bksgc->bktgc", kernel, wide_x, precision=highest)
        local_back = jnp.einsum("gts,bktgc->bksgc", kernel, wide_d, precision=highest)
        pairs = jnp.einsum("bktgc,bksgc->gts", half_d, half_x, preferred_element_type=jnp.float32)
        pairs = jnp.where(causal_mask, pairs, 0.0)
        local_grad = weight_piece * jnp.einsum(
            "gmt,gts,gms->gm", down_piece, pairs, up_piece, precision=highest
        )
        return (local_out, local_back, local_grad)

    half_inputs = inputs.reshape(five_shape)
    half_cotangent = cotangent.reshape(five_shape)
    block_out, block_back, block_grad = lax.map(
        local_block,
        (
            by_groups(coefficient),
            by_groups(decay_down),
            by_groups(decay_up),
            by_groups(weight),
            data_blocks(inputs_wide),
            data_blocks(cotangent_wide),
            data_blocks(half_inputs),
            data_blocks(half_cotangent),
        ),
    )
    local_out = block_out.transpose(1, 2, 3, 0, 4, 5).reshape(five_shape)
    local_back = block_back.transpose(1, 2, 3, 0, 4, 5).reshape(five_shape)
    local_grad = block_grad.reshape(group_count, mode_count)
    running = state_before.reshape(state_split)
    before_list = [running]
    running = state_after.reshape(state_split)
    after_list = [None] * sub_count
    after_list[0] = running
    before_stack = jnp.stack(before_list, axis=1)
    after_stack = jnp.stack(after_list, axis=1)
    first_weights = coefficient[:, :, None] * jnp.exp(-rate_cube * (positions + 1.0))
    last_weights = coefficient[:, :, None] * jnp.exp(-rate_cube * (sub_rows - positions))
    carried_out = jnp.einsum("gmt,bkmgc->bktgc", first_weights, before_stack, precision=highest)
    carried_back = jnp.einsum("gmt,bkmgc->bktgc", last_weights, after_stack, precision=highest)
    carried_grad = (
        weight
        * jnp.exp(-decay_rates)
        * jnp.einsum("kbmgc,bkmgc->gm", sub_starts, before_stack, precision=highest)
    )
    skip_wide = skip_gain.reshape(group_count, group_width)
    outputs = (
        (local_out + carried_out + skip_wide * inputs_wide)
        .reshape(local_batch, block_rows, channels)
        .astype(jnp.bfloat16)
    )
    grad_inputs = (
        (local_back + carried_back + skip_wide * cotangent_wide)
        .reshape(local_batch, block_rows, channels)
        .astype(jnp.bfloat16)
    )
    token_total = local_batch * block_rows * lax.axis_size("dp") * lax.axis_size("ctx")
    scale = 1.0 / math.sqrt(token_total)
    skip_local = jnp.sum(inputs_wide * cotangent_wide, axis=(0, 1, 2)).reshape(channels)
    grad_residues, grad_skip = lax.psum(
        ((local_grad + carried_grad) * scale, skip_local * scale), ("dp", "ctx")
    )
    return (outputs, grad_inputs, grad_residues, grad_skip)


def solution(mesh):
    placed = (P("dp", "ctx", "tp"), P("dp", "ctx", "tp"), P("tp", None), P("tp", None), P("tp"))
    return jax.shard_map(
        shards,
        mesh=mesh,
        in_specs=placed,
        out_specs=(P("dp", "ctx", "tp"), P("dp", "ctx", "tp"), P("tp", None), P("tp")),
        check_vma=False,
    )
```

profile of v0, /device:TPU:16, one launch (start us, length us, event | category | flops | bytes accessed | tf_op | source)
XLA Modules:
  0.0 629.1 jit_solution(2040821487755064121)
XLA Ops:
  6.7 172.4 %while.30 = (s32[]{:T(128)}, f32[16,1,1,256,4,16]{3,5,4,2,1,0:T(8,128)}, f32[16,1,1,256,4,16]{3,5,4,2,1,0:T(8,128)}, f32[16,4,16]{2,1,0:T(4,128)S(1)}, f32[16,1,...) while((s32[]{:T(128)}, ...), condition=%wide.region_1.0_spmd.clone.clone, body=%wide.region_0.0_spmd.clone.clone.sunk | while | flops 210354176 | bytes 6303369 | solution.py:85
  184.8 158.3 %while.29 = (s32[]{:T(128)}, f32[1,16,1024]{2,1,0:T(8,128)S(1)}, f32[1,16,1024]{2,1,0:T(8,128)S(1)}, f32[1,16,1024]{2,1,0:T(8,128)S(1)}, f32[1,16,1024]{2,1,0:T(8,128)S(1)}, /*index=5*/f32[16,64]{1,0:T(8,128)S(1)}, s32[]{:T(128)}) while((s32[]{:T(128)}, f32[1,16,1024]{2,1,0:T(8,128)S(1)}, f32[1,16,1024]{2,1,0:T(8,128)S(1)}, ...), condition=%wide.region_3.4_spmd.clone, body=%wide.region_2.3_spmd.clone.sunk | while | flops 65538 | bytes 1183901 | solution.py:52
  185.3 3.8 collective-permute-start
  191.0 4.3 collective-permute-done.1
  195.8 3.8 collective-permute-start
  201.5 5.3 collective-permute-done.1
  207.3 5.1 collective-permute-start
  214.3 4.3 collective-permute-done.1
  219.1 3.9 collective-permute-start
  224.9 4.3 collective-permute-done.1
  229.7 4.8 collective-permute-start
  236.3 4.3 collective-permute-done.1
  241.1 5.1 collective-permute-start
  248.1 4.3 collective-permute-done.1
  252.9 3.9 collective-permute-start
  259.0 4.4 collective-permute-done.1
  263.9 3.9 collective-permute-start
  269.7 4.3 collective-permute-done.1
  279.2 4.3 collective-permute-done.1
  284.0 3.3 collective-permute-start
  289.2 4.3 collective-permute-done.1
  293.9 3.1 collective-permute-start
  299.0 4.3 collective-permute-done.1
  303.7 3.3 collective-permute-start
  308.9 4.3 collective-permute-done.1
  313.7 3.4 collective-permute-start
  319.1 4.6 collective-permute-done.1
  324.2 3.4 collective-permute-start
  329.5 4.3 collective-permute-done.1
  338.9 4.3 collective-permute-done.1
  343.9 3.3 fusion.34
  353.2 275.2 %all-reduce = (f32[64,16]{1,0:T(8,128)S(1)}, f32[1024]{0:T(1024)}) all-reduce(f32[64,16]{1,0:T(8,128)S(1)} %add_multiply_fusion, f32[1024]{0:T(1024)S(1)} %broadcast_multiply_fusion), channel_id=1, replica_groups=mesh['dp'=4,'ctx'=16,'tp'=8] {'dp','ctx'}, use_global_device_ids=true, to_apply=%region_4.5 | all-reduce | flops 2048 | bytes 16384 | tf_op jit(solution)/shard_map/psum | solution.py:131
  (289 shorter events, 231.8 us)
Async XLA Ops:
  1.6 1.7 copy-start
  3.3 1.2 copy-start.1
  185.3 5.7 collective-permute-start
  189.1 6.2 collective-permute-start.1
  195.8 5.7 collective-permute-start
  199.6 7.2 %collective-permute-start.1 = (f32[1,16,1024]{2,1,0:T(8,128)S(1)}, f32[1,16,1024]{2,1,0:T(8,128)S(1)}, u32[]{:S(2)}, u32[]{:S(2)}) collective-permute-start(f32[1,16,1024]{2,1,0:T(8,128)S(1)} %get-tuple-element.351), channel_id=1, source_target_pairs={{8,0},{16,8},{24,16},{32,24},{40,32},{48,40},{56,48},{64,56},{72,6... | collective-permute-start | bytes 196616 | tf_op jit(solution)/shard_map/while/body/eval_jaxpr/ppermute | solution.py:13
  207.3 7.0 %collective-permute-start = (f32[1,16,1024]{2,1,0:T(8,128)S(1)}, f32[1,16,1024]{2,1,0:T(8,128)S(1)}, u32[]{:S(2)}, u32[]{:S(2)}) collective-permute-start(f32[1,16,1024]{2,1,0:T(8,128)S(1)} %get-tuple-element.350), channel_id=1, source_target_pairs={{0,8},{8,16},{16,24},{24,32},{32,40},{40,48},{48,56},{56,64},{64,7... | collective-permute-start | bytes 196616 | tf_op jit(solution)/shard_map/while/body/eval_jaxpr/ppermute | solution.py:13
  212.4 6.2 collective-permute-start.1
  219.1 5.8 collective-permute-start
  223.0 6.2 collective-permute-start.1
  229.7 6.6 %collective-permute-start = (f32[1,16,1024]{2,1,0:T(8,128)S(1)}, f32[1,16,1024]{2,1,0:T(8,128)S(1)}, u32[]{:S(2)}, u32[]{:S(2)}) collective-permute-start(f32[1,16,1024]{2,1,0:T(8,128)S(1)} %get-tuple-element.350), channel_id=1, source_target_pairs={{0,8},{8,16},{16,24},{24,32},{32,40},{40,48},{48,56},{56,64},{64,7... | collective-permute-start | bytes 196616 | tf_op jit(solution)/shard_map/while/body/eval_jaxpr/ppermute | solution.py:13
  234.4 6.2 collective-permute-start.1
  241.1 7.0 %collective-permute-start = (f32[1,16,1024]{2,1,0:T(8,128)S(1)}, f32[1,16,1024]{2,1,0:T(8,128)S(1)}, u32[]{:S(2)}, u32[]{:S(2)}) collective-permute-start(f32[1,16,1024]{2,1,0:T(8,128)S(1)} %get-tuple-element.350), channel_id=1, source_target_pairs={{0,8},{8,16},{16,24},{24,32},{32,40},{40,48},{48,56},{56,64},{64,7... | collective-permute-start | bytes 196616 | tf_op jit(solution)/shard_map/while/body/eval_jaxpr/ppermute | solution.py:13
  246.2 6.2 collective-permute-start.1
  252.9 6.1 collective-permute-start
  256.8 6.6 %collective-permute-start.1 = (f32[1,16,1024]{2,1,0:T(8,128)S(1)}, f32[1,16,1024]{2,1,0:T(8,128)S(1)}, u32[]{:S(2)}, u32[]{:S(2)}) collective-permute-start(f32[1,16,1024]{2,1,0:T(8,128)S(1)} %get-tuple-element.351), channel_id=1, source_target_pairs={{8,0},{16,8},{24,16},{32,24},{40,32},{48,40},{56,48},{64,56},{72,6... | collective-permute-start | bytes 196616 | tf_op jit(solution)/shard_map/while/body/eval_jaxpr/ppermute | solution.py:13
  263.9 5.8 collective-permute-start
  267.8 6.2 collective-permute-start.1
  274.5 4.7 collective-permute-start
  277.3 6.2 collective-permute-start.1
  284.0 5.2 collective-permute-start
  287.3 6.2 collective-permute-start.1
  293.9 5.0 collective-permute-start
  297.1 6.2 collective-permute-start.1
  303.7 5.2 collective-permute-start
  307.0 6.2 collective-permute-start.1
  313.7 5.4 collective-permute-start
  317.1 6.5 %collective-permute-start.1 = (f32[1,16,1024]{2,1,0:T(8,128)S(1)}, f32[1,16,1024]{2,1,0:T(8,128)S(1)}, u32[]{:S(2)}, u32[]{:S(2)}) collective-permute-start(f32[1,16,1024]{2,1,0:T(8,128)S(1)} %get-tuple-element.351), channel_id=1, source_target_pairs={{8,0},{16,8},{24,16},{32,24},{40,32},{48,40},{56,48},{64,56},{72,6... | collective-permute-start | bytes 196616 | tf_op jit(solution)/shard_map/while/body/eval_jaxpr/ppermute | solution.py:13
  324.2 5.3 collective-permute-start
  327.6 6.2 collective-permute-start.1
  334.2 4.6 collective-permute-start
  337.0 6.2 collective-permute-start.1
  (6 other events, 5.1 us)
where the time goes:
time: 634 us; the launch traced here: 629 us
  blocking collectives  275 us (43%)
  matrix products  163 us (26%)
  starting transfers between devices  75.9 us (12%)
  waiting for transfers between devices  74.7 us (12%)
  local copies, waits for them, and re-layouts  34.5 us (5%)
    psum x1, blocking collectives, shards(): lax.psum(((local_grad + carried_grad) * scale, skip_local * scale), ('dp'...  275 us
    ppermute x30, starting transfers between devices, passed_along(): return lax.ppermute(value, axis, pairs)  75.9 us
    ppermute x30, waiting for transfers between devices, passed_along(): return lax.ppermute(value, axis, pairs)  74.7 us
    dot_general x16, matrix products, local_block(): jnp.einsum('gmt,gts,gms->gm', down_piece, pairs, up_piece, precision=high...  43.6 us
    dot_general x16, matrix products, local_block(): jnp.einsum('gts,bksgc->bktgc', kernel, wide_x, precision=highest)  39.2 us
    dot_general x16, matrix products, local_block(): jnp.einsum('gm,gmt,gms->gts', coef_piece, down_piece, up_piece, precision...  32.7 us
    dot_general x16, matrix products, local_block(): jnp.einsum('gts,bktgc->bksgc', kernel, wide_d, precision=highest)  19.9 us
    dot_general x16, matrix products, local_block(): jnp.einsum('bktgc,bksgc->gts', half_d, half_x, preferred_element_type=jnp...  17.8 us
  transfers between devices with their start and end apart: 30, of which 30 were waited for; matrix products, arithmetic and copies ran while one was open for 0% of the time, Pallas kernels for 0%

commit v1 on v0

--- a/solution.py
+++ b/solution.py
@@ -129,7 +129,7 @@
     scale = 1.0 / math.sqrt(token_total)
     skip_local = jnp.sum(inputs_wide * cotangent_wide, axis=(0, 1, 2)).reshape(channels)
     grad_residues, grad_skip = lax.psum(
-        ((local_grad + carried_grad) * scale, skip_local * scale), ("dp", "ctx")
+        lax.psum(((local_grad + carried_grad) * scale, skip_local * scale), "ctx"), "dp"
     )
     return (outputs, grad_inputs, grad_residues, grad_skip)
 

time: 634 us -> 430 us (0.68)
  the two profiles are of different devices: /device:TPU:16 before, /device:TPU:8 now
where the time goes in v1:
time: 430 us; the launch traced here: 425 us
  matrix products  163 us (38%)
  starting transfers between devices  76 us (18%)
  waiting for transfers between devices  74.6 us (17%)
  blocking collectives  71.7 us (17%)
  local copies, waits for them, and re-layouts  33.9 us (8%)
    ppermute x30, starting transfers between devices, passed_along(): return lax.ppermute(value, axis, pairs)  76 us
    ppermute x30, waiting for transfers between devices, passed_along(): return lax.ppermute(value, axis, pairs)  74.6 us
    psum x1, blocking collectives, shards(): lax.psum(((local_grad + carried_grad) * scale, skip_local * scale), 'ctx')  53.8 us
    dot_general x16, matrix products, local_block(): jnp.einsum('gmt,gts,gms->gm', down_piece, pairs, up_piece, precision=high...  43.6 us
    dot_general x16, matrix products, local_block(): jnp.einsum('gts,bksgc->bktgc', kernel, wide_x, precision=highest)  39.2 us
    dot_general x16, matrix products, local_block(): jnp.einsum('gm,gmt,gms->gts', coef_piece, down_piece, up_piece, precision...  32.7 us
    dot_general x16, matrix products, local_block(): jnp.einsum('gts,bktgc->bksgc', kernel, wide_d, precision=highest)  19.9 us
    psum x1, blocking collectives, shards(): lax.psum(lax.psum(((local_grad + carried_grad) * scale, skip_local * scal...  17.9 us
  transfers between devices with their start and end apart: 30, of which 30 were waited for; matrix products, arithmetic and copies ran while one was open for 0% of the time, Pallas kernels for 0%

profile of v1, /device:TPU:8, one launch (start us, length us, event | category | flops | bytes accessed | tf_op | source)
XLA Modules:
  0.0 425.0 jit_solution(14888512903051407676)
XLA Ops:
  6.7 172.4 %while.30 = (s32[]{:T(128)}, f32[16,1,1,256,4,16]{3,5,4,2,1,0:T(8,128)}, f32[16,1,1,256,4,16]{3,5,4,2,1,0:T(8,128)}, f32[16,4,16]{2,1,0:T(4,128)S(1)}, f32[16,1,...) while((s32[]{:T(128)}, ...), condition=%wide.region_1.0_spmd.clone.clone, body=%wide.region_0.0_spmd.clone.clone.sunk | while | flops 210354176 | bytes 6303369 | solution.py:85
  184.0 158.4 %while.29 = (s32[]{:T(128)}, f32[1,16,1024]{2,1,0:T(8,128)S(1)}, f32[1,16,1024]{2,1,0:T(8,128)S(1)}, f32[1,16,1024]{2,1,0:T(8,128)S(1)}, f32[1,16,1024]{2,1,0:T(8,128)S(1)}, /*index=5*/f32[16,64]{1,0:T(8,128)S(1)}, s32[]{:T(128)}) while((s32[]{:T(128)}, f32[1,16,1024]{2,1,0:T(8,128)S(1)}, f32[1,16,1024]{2,1,0:T(8,128)S(1)}, ...), condition=%wide.region_3.4_spmd.clone, body=%wide.region_2.3_spmd.clone.sunk | while | flops 65538 | bytes 1183901 | solution.py:52
  184.5 3.8 collective-permute-start
  190.2 4.3 %collective-permute-done.1 = f32[1,16,1024]{2,1,0:T(8,128)S(1)} collective-permute-done((f32[1,16,1024]{2,1,0:T(8,128)S(1)}, f32[1,16,1024]{2,1,0:T(8,128)S(1)}, u32[]{:S(2)}, u32[]{:S(2)}) %collective-permute-start.1) | collective-permute-done | bytes 65568 | tf_op jit(solution)/shard_map/while/body/eval_jaxpr/ppermute | solution.py:13
  195.0 3.8 collective-permute-start
  200.7 5.3 %collective-permute-done.1 = f32[1,16,1024]{2,1,0:T(8,128)S(1)} collective-permute-done((f32[1,16,1024]{2,1,0:T(8,128)S(1)}, f32[1,16,1024]{2,1,0:T(8,128)S(1)}, u32[]{:S(2)}, u32[]{:S(2)}) %collective-permute-start.1) | collective-permute-done | bytes 65568 | tf_op jit(solution)/shard_map/while/body/eval_jaxpr/ppermute | solution.py:13
  206.5 5.1 %collective-permute-start = (f32[1,16,1024]{2,1,0:T(8,128)S(1)}, f32[1,16,1024]{2,1,0:T(8,128)S(1)}, u32[]{:S(2)}, u32[]{:S(2)}) collective-permute-start(f32[1,16,1024]{2,1,0:T(8,128)S(1)} %get-tuple-element.352), channel_id=1, source_target_pairs={{0,8},{8,16},{16,24},{24,32},{32,40},{40,48},{48,56},{56,64},{64,7... | collective-permute-start | bytes 196616 | tf_op jit(solution)/shard_map/while/body/eval_jaxpr/ppermute | solution.py:13
  213.5 4.3 %collective-permute-done.1 = f32[1,16,1024]{2,1,0:T(8,128)S(1)} collective-permute-done((f32[1,16,1024]{2,1,0:T(8,128)S(1)}, f32[1,16,1024]{2,1,0:T(8,128)S(1)}, u32[]{:S(2)}, u32[]{:S(2)}) %collective-permute-start.1) | collective-permute-done | bytes 65568 | tf_op jit(solution)/shard_map/while/body/eval_jaxpr/ppermute | solution.py:13
  218.3 3.9 collective-permute-start
  224.1 4.3 %collective-permute-done.1 = f32[1,16,1024]{2,1,0:T(8,128)S(1)} collective-permute-done((f32[1,16,1024]{2,1,0:T(8,128)S(1)}, f32[1,16,1024]{2,1,0:T(8,128)S(1)}, u32[]{:S(2)}, u32[]{:S(2)}) %collective-permute-start.1) | collective-permute-done | bytes 65568 | tf_op jit(solution)/shard_map/while/body/eval_jaxpr/ppermute | solution.py:13
  228.9 4.8 %collective-permute-start = (f32[1,16,1024]{2,1,0:T(8,128)S(1)}, f32[1,16,1024]{2,1,0:T(8,128)S(1)}, u32[]{:S(2)}, u32[]{:S(2)}) collective-permute-start(f32[1,16,1024]{2,1,0:T(8,128)S(1)} %get-tuple-element.352), channel_id=1, source_target_pairs={{0,8},{8,16},{16,24},{24,32},{32,40},{40,48},{48,56},{56,64},{64,7... | collective-permute-start | bytes 196616 | tf_op jit(solution)/shard_map/while/body/eval_jaxpr/ppermute | solution.py:13
  235.6 4.3 %collective-permute-done.1 = f32[1,16,1024]{2,1,0:T(8,128)S(1)} collective-permute-done((f32[1,16,1024]{2,1,0:T(8,128)S(1)}, f32[1,16,1024]{2,1,0:T(8,128)S(1)}, u32[]{:S(2)}, u32[]{:S(2)}) %collective-permute-start.1) | collective-permute-done | bytes 65568 | tf_op jit(solution)/shard_map/while/body/eval_jaxpr/ppermute | solution.py:13
  240.3 5.1 %collective-permute-start = (f32[1,16,1024]{2,1,0:T(8,128)S(1)}, f32[1,16,1024]{2,1,0:T(8,128)S(1)}, u32[]{:S(2)}, u32[]{:S(2)}) collective-permute-start(f32[1,16,1024]{2,1,0:T(8,128)S(1)} %get-tuple-element.352), channel_id=1, source_target_pairs={{0,8},{8,16},{16,24},{24,32},{32,40},{40,48},{48,56},{56,64},{64,7... | collective-permute-start | bytes 196616 | tf_op jit(solution)/shard_map/while/body/eval_jaxpr/ppermute | solution.py:13
  247.4 4.3 %collective-permute-done.1 = f32[1,16,1024]{2,1,0:T(8,128)S(1)} collective-permute-done((f32[1,16,1024]{2,1,0:T(8,128)S(1)}, f32[1,16,1024]{2,1,0:T(8,128)S(1)}, u32[]{:S(2)}, u32[]{:S(2)}) %collective-permute-start.1) | collective-permute-done | bytes 65568 | tf_op jit(solution)/shard_map/while/body/eval_jaxpr/ppermute | solution.py:13
  252.1 3.9 collective-permute-start
  258.3 4.3 %collective-permute-done.1 = f32[1,16,1024]{2,1,0:T(8,128)S(1)} collective-permute-done((f32[1,16,1024]{2,1,0:T(8,128)S(1)}, f32[1,16,1024]{2,1,0:T(8,128)S(1)}, u32[]{:S(2)}, u32[]{:S(2)}) %collective-permute-start.1) | collective-permute-done | bytes 65568 | tf_op jit(solution)/shard_map/while/body/eval_jaxpr/ppermute | solution.py:13
  263.1 3.9 collective-permute-start
  268.9 4.3 %collective-permute-done.1 = f32[1,16,1024]{2,1,0:T(8,128)S(1)} collective-permute-done((f32[1,16,1024]{2,1,0:T(8,128)S(1)}, f32[1,16,1024]{2,1,0:T(8,128)S(1)}, u32[]{:S(2)}, u32[]{:S(2)}) %collective-permute-start.1) | collective-permute-done | bytes 65568 | tf_op jit(solution)/shard_map/while/body/eval_jaxpr/ppermute | solution.py:13
  278.4 4.3 %collective-permute-done.1 = f32[1,16,1024]{2,1,0:T(8,128)S(1)} collective-permute-done((f32[1,16,1024]{2,1,0:T(8,128)S(1)}, f32[1,16,1024]{2,1,0:T(8,128)S(1)}, u32[]{:S(2)}, u32[]{:S(2)}) %collective-permute-start.1) | collective-permute-done | bytes 65568 | tf_op jit(solution)/shard_map/while/body/eval_jaxpr/ppermute | solution.py:13
  283.2 3.3 collective-permute-start
  288.4 4.3 %collective-permute-done.1 = f32[1,16,1024]{2,1,0:T(8,128)S(1)} collective-permute-done((f32[1,16,1024]{2,1,0:T(8,128)S(1)}, f32[1,16,1024]{2,1,0:T(8,128)S(1)}, u32[]{:S(2)}, u32[]{:S(2)}) %collective-permute-start.1) | collective-permute-done | bytes 65568 | tf_op jit(solution)/shard_map/while/body/eval_jaxpr/ppermute | solution.py:13
  298.2 4.3 %collective-permute-done.1 = f32[1,16,1024]{2,1,0:T(8,128)S(1)} collective-permute-done((f32[1,16,1024]{2,1,0:T(8,128)S(1)}, f32[1,16,1024]{2,1,0:T(8,128)S(1)}, u32[]{:S(2)}, u32[]{:S(2)}) %collective-permute-start.1) | collective-permute-done | bytes 65568 | tf_op jit(solution)/shard_map/while/body/eval_jaxpr/ppermute | solution.py:13
  302.9 3.3 collective-permute-start
  308.2 4.3 %collective-permute-done.1 = f32[1,16,1024]{2,1,0:T(8,128)S(1)} collective-permute-done((f32[1,16,1024]{2,1,0:T(8,128)S(1)}, f32[1,16,1024]{2,1,0:T(8,128)S(1)}, u32[]{:S(2)}, u32[]{:S(2)}) %collective-permute-start.1) | collective-permute-done | bytes 65568 | tf_op jit(solution)/shard_map/while/body/eval_jaxpr/ppermute | solution.py:13
  312.9 3.4 collective-permute-start
  318.3 4.6 %collective-permute-done.1 = f32[1,16,1024]{2,1,0:T(8,128)S(1)} collective-permute-done((f32[1,16,1024]{2,1,0:T(8,128)S(1)}, f32[1,16,1024]{2,1,0:T(8,128)S(1)}, u32[]{:S(2)}, u32[]{:S(2)}) %collective-permute-start.1) | collective-permute-done | bytes 65568 | tf_op jit(solution)/shard_map/while/body/eval_jaxpr/ppermute | solution.py:13
  323.4 3.4 collective-permute-start
  328.7 4.3 %collective-permute-done.1 = f32[1,16,1024]{2,1,0:T(8,128)S(1)} collective-permute-done((f32[1,16,1024]{2,1,0:T(8,128)S(1)}, f32[1,16,1024]{2,1,0:T(8,128)S(1)}, u32[]{:S(2)}, u32[]{:S(2)}) %collective-permute-start.1) | collective-permute-done | bytes 65568 | tf_op jit(solution)/shard_map/while/body/eval_jaxpr/ppermute | solution.py:13
  338.1 4.3 %collective-permute-done.1 = f32[1,16,1024]{2,1,0:T(8,128)S(1)} collective-permute-done((f32[1,16,1024]{2,1,0:T(8,128)S(1)}, f32[1,16,1024]{2,1,0:T(8,128)S(1)}, u32[]{:S(2)}, u32[]{:S(2)}) %collective-permute-start.1) | collective-permute-done | bytes 65568 | tf_op jit(solution)/shard_map/while/body/eval_jaxpr/ppermute | solution.py:13
  343.9 53.8 %all-reduce = (f32[64,16]{1,0:T(8,128)S(1)}, f32[1024]{0:T(1024)S(1)}) all-reduce(f32[64,16]{1,0:T(8,128)S(1)} %add_multiply_fusion, f32[1024]{0:T(1024)S(1)} %broadcast_multiply_fusion), channel_id=1, replica_groups=mesh['dp'=4,'ctx'=16,'tp'=8] {'ctx'}, use_global_device_ids=true, to_apply=%region_4.5 | all-reduce | flops 2048 | bytes 16384 | tf_op jit(solution)/shard_map/psum | solution.py:132
  397.7 17.9 %all-reduce.1 = (f32[64,16]{1,0:T(8,128)S(1)}, f32[1024]{0:T(1024)}) all-reduce(f32[64,16]{1,0:T(8,128)S(1)} %get-tuple-element.241, f32[1024]{0:T(1024)S(1)} %get-tuple-element.242), channel_id=1, replica_groups=mesh['dp'=4,'ctx'=16,'tp'=8] {'dp'}, use_global_device_ids=true, to_apply=%region_5.6 | all-reduce | flops 2048 | bytes 16384 | tf_op jit(solution)/shard_map/psum | solution.py:131
  417.0 3.3 fusion.34
  (286 shorter events, 234.3 us)
Async XLA Ops:
  1.6 1.7 copy-start
  3.3 1.2 copy-start.1
  184.5 5.7 %collective-permute-start = (f32[1,16,1024]{2,1,0:T(8,128)S(1)}, f32[1,16,1024]{2,1,0:T(8,128)S(1)}, u32[]{:S(2)}, u32[]{:S(2)}) collective-permute-start(f32[1,16,1024]{2,1,0:T(8,128)S(1)} %get-tuple-element.352), channel_id=1, source_target_pairs={{0,8},{8,16},{16,24},{24,32},{32,40},{40,48},{48,56},{56,64},{64,7... | collective-permute-start | bytes 196616 | tf_op jit(solution)/shard_map/while/body/eval_jaxpr/ppermute | solution.py:13
  188.4 6.2 %collective-permute-start.1 = (f32[1,16,1024]{2,1,0:T(8,128)S(1)}, f32[1,16,1024]{2,1,0:T(8,128)S(1)}, u32[]{:S(2)}, u32[]{:S(2)}) collective-permute-start(f32[1,16,1024]{2,1,0:T(8,128)S(1)} %get-tuple-element.353), channel_id=1, source_target_pairs={{8,0},{16,8},{24,16},{32,24},{40,32},{48,40},{56,48},{64,56},{72,6... | collective-permute-start | bytes 196616 | tf_op jit(solution)/shard_map/while/body/eval_jaxpr/ppermute | solution.py:13
  195.0 5.7 %collective-permute-start = (f32[1,16,1024]{2,1,0:T(8,128)S(1)}, f32[1,16,1024]{2,1,0:T(8,128)S(1)}, u32[]{:S(2)}, u32[]{:S(2)}) collective-permute-start(f32[1,16,1024]{2,1,0:T(8,128)S(1)} %get-tuple-element.352), channel_id=1, source_target_pairs={{0,8},{8,16},{16,24},{24,32},{32,40},{40,48},{48,56},{56,64},{64,7... | collective-permute-start | bytes 196616 | tf_op jit(solution)/shard_map/while/body/eval_jaxpr/ppermute | solution.py:13
  198.9 7.2 %collective-permute-start.1 = (f32[1,16,1024]{2,1,0:T(8,128)S(1)}, f32[1,16,1024]{2,1,0:T(8,128)S(1)}, u32[]{:S(2)}, u32[]{:S(2)}) collective-permute-start(f32[1,16,1024]{2,1,0:T(8,128)S(1)} %get-tuple-element.353), channel_id=1, source_target_pairs={{8,0},{16,8},{24,16},{32,24},{40,32},{48,40},{56,48},{64,56},{72,6... | collective-permute-start | bytes 196616 | tf_op jit(solution)/shard_map/while/body/eval_jaxpr/ppermute | solution.py:13
  206.5 7.0 %collective-permute-start = (f32[1,16,1024]{2,1,0:T(8,128)S(1)}, f32[1,16,1024]{2,1,0:T(8,128)S(1)}, u32[]{:S(2)}, u32[]{:S(2)}) collective-permute-start(f32[1,16,1024]{2,1,0:T(8,128)S(1)} %get-tuple-element.352), channel_id=1, source_target_pairs={{0,8},{8,16},{16,24},{24,32},{32,40},{40,48},{48,56},{56,64},{64,7... | collective-permute-start | bytes 196616 | tf_op jit(solution)/shard_map/while/body/eval_jaxpr/ppermute | solution.py:13
  211.7 6.2 %collective-permute-start.1 = (f32[1,16,1024]{2,1,0:T(8,128)S(1)}, f32[1,16,1024]{2,1,0:T(8,128)S(1)}, u32[]{:S(2)}, u32[]{:S(2)}) collective-permute-start(f32[1,16,1024]{2,1,0:T(8,128)S(1)} %get-tuple-element.353), channel_id=1, source_target_pairs={{8,0},{16,8},{24,16},{32,24},{40,32},{48,40},{56,48},{64,56},{72,6... | collective-permute-start | bytes 196616 | tf_op jit(solution)/shard_map/while/body/eval_jaxpr/ppermute | solution.py:13
  218.3 5.8 %collective-permute-start = (f32[1,16,1024]{2,1,0:T(8,128)S(1)}, f32[1,16,1024]{2,1,0:T(8,128)S(1)}, u32[]{:S(2)}, u32[]{:S(2)}) collective-permute-start(f32[1,16,1024]{2,1,0:T(8,128)S(1)} %get-tuple-element.352), channel_id=1, source_target_pairs={{0,8},{8,16},{16,24},{24,32},{32,40},{40,48},{48,56},{56,64},{64,7... | collective-permute-start | bytes 196616 | tf_op jit(solution)/shard_map/while/body/eval_jaxpr/ppermute | solution.py:13
  222.2 6.2 %collective-permute-start.1 = (f32[1,16,1024]{2,1,0:T(8,128)S(1)}, f32[1,16,1024]{2,1,0:T(8,128)S(1)}, u32[]{:S(2)}, u32[]{:S(2)}) collective-permute-start(f32[1,16,1024]{2,1,0:T(8,128)S(1)} %get-tuple-element.353), channel_id=1, source_target_pairs={{8,0},{16,8},{24,16},{32,24},{40,32},{48,40},{56,48},{64,56},{72,6... | collective-permute-start | bytes 196616 | tf_op jit(solution)/shard_map/while/body/eval_jaxpr/ppermute | solution.py:13
  228.9 6.7 %collective-permute-start = (f32[1,16,1024]{2,1,0:T(8,128)S(1)}, f32[1,16,1024]{2,1,0:T(8,128)S(1)}, u32[]{:S(2)}, u32[]{:S(2)}) collective-permute-start(f32[1,16,1024]{2,1,0:T(8,128)S(1)} %get-tuple-element.352), channel_id=1, source_target_pairs={{0,8},{8,16},{16,24},{24,32},{32,40},{40,48},{48,56},{56,64},{64,7... | collective-permute-start | bytes 196616 | tf_op jit(solution)/shard_map/while/body/eval_jaxpr/ppermute | solution.py:13
  233.7 6.2 %collective-permute-start.1 = (f32[1,16,1024]{2,1,0:T(8,128)S(1)}, f32[1,16,1024]{2,1,0:T(8,128)S(1)}, u32[]{:S(2)}, u32[]{:S(2)}) collective-permute-start(f32[1,16,1024]{2,1,0:T(8,128)S(1)} %get-tuple-element.353), channel_id=1, source_target_pairs={{8,0},{16,8},{24,16},{32,24},{40,32},{48,40},{56,48},{64,56},{72,6... | collective-permute-start | bytes 196616 | tf_op jit(solution)/shard_map/while/body/eval_jaxpr/ppermute | solution.py:13
  240.3 7.0 %collective-permute-start = (f32[1,16,1024]{2,1,0:T(8,128)S(1)}, f32[1,16,1024]{2,1,0:T(8,128)S(1)}, u32[]{:S(2)}, u32[]{:S(2)}) collective-permute-start(f32[1,16,1024]{2,1,0:T(8,128)S(1)} %get-tuple-element.352), channel_id=1, source_target_pairs={{0,8},{8,16},{16,24},{24,32},{32,40},{40,48},{48,56},{56,64},{64,7... | collective-permute-start | bytes 196616 | tf_op jit(solution)/shard_map/while/body/eval_jaxpr/ppermute | solution.py:13
  245.5 6.2 %collective-permute-start.1 = (f32[1,16,1024]{2,1,0:T(8,128)S(1)}, f32[1,16,1024]{2,1,0:T(8,128)S(1)}, u32[]{:S(2)}, u32[]{:S(2)}) collective-permute-start(f32[1,16,1024]{2,1,0:T(8,128)S(1)} %get-tuple-element.353), channel_id=1, source_target_pairs={{8,0},{16,8},{24,16},{32,24},{40,32},{48,40},{56,48},{64,56},{72,6... | collective-permute-start | bytes 196616 | tf_op jit(solution)/shard_map/while/body/eval_jaxpr/ppermute | solution.py:13
  252.1 6.1 %collective-permute-start = (f32[1,16,1024]{2,1,0:T(8,128)S(1)}, f32[1,16,1024]{2,1,0:T(8,128)S(1)}, u32[]{:S(2)}, u32[]{:S(2)}) collective-permute-start(f32[1,16,1024]{2,1,0:T(8,128)S(1)} %get-tuple-element.352), channel_id=1, source_target_pairs={{0,8},{8,16},{16,24},{24,32},{32,40},{40,48},{48,56},{56,64},{64,7... | collective-permute-start | bytes 196616 | tf_op jit(solution)/shard_map/while/body/eval_jaxpr/ppermute | solution.py:13
  256.1 6.6 %collective-permute-start.1 = (f32[1,16,1024]{2,1,0:T(8,128)S(1)}, f32[1,16,1024]{2,1,0:T(8,128)S(1)}, u32[]{:S(2)}, u32[]{:S(2)}) collective-permute-start(f32[1,16,1024]{2,1,0:T(8,128)S(1)} %get-tuple-element.353), channel_id=1, source_target_pairs={{8,0},{16,8},{24,16},{32,24},{40,32},{48,40},{56,48},{64,56},{72,6... | collective-permute-start | bytes 196616 | tf_op jit(solution)/shard_map/while/body/eval_jaxpr/ppermute | solution.py:13
  263.1 5.8 %collective-permute-start = (f32[1,16,1024]{2,1,0:T(8,128)S(1)}, f32[1,16,1024]{2,1,0:T(8,128)S(1)}, u32[]{:S(2)}, u32[]{:S(2)}) collective-permute-start(f32[1,16,1024]{2,1,0:T(8,128)S(1)} %get-tuple-element.352), channel_id=1, source_target_pairs={{0,8},{8,16},{16,24},{24,32},{32,40},{40,48},{48,56},{56,64},{64,7... | collective-permute-start | bytes 196616 | tf_op jit(solution)/shard_map/while/body/eval_jaxpr/ppermute | solution.py:13
  267.0 6.2 %collective-permute-start.1 = (f32[1,16,1024]{2,1,0:T(8,128)S(1)}, f32[1,16,1024]{2,1,0:T(8,128)S(1)}, u32[]{:S(2)}, u32[]{:S(2)}) collective-permute-start(f32[1,16,1024]{2,1,0:T(8,128)S(1)} %get-tuple-element.353), channel_id=1, source_target_pairs={{8,0},{16,8},{24,16},{32,24},{40,32},{48,40},{56,48},{64,56},{72,6... | collective-permute-start | bytes 196616 | tf_op jit(solution)/shard_map/while/body/eval_jaxpr/ppermute | solution.py:13
  273.7 4.7 %collective-permute-start = (f32[1,16,1024]{2,1,0:T(8,128)S(1)}, f32[1,16,1024]{2,1,0:T(8,128)S(1)}, u32[]{:S(2)}, u32[]{:S(2)}) collective-permute-start(f32[1,16,1024]{2,1,0:T(8,128)S(1)} %get-tuple-element.352), channel_id=1, source_target_pairs={{0,8},{8,16},{16,24},{24,32},{32,40},{40,48},{48,56},{56,64},{64,7... | collective-permute-start | bytes 196616 | tf_op jit(solution)/shard_map/while/body/eval_jaxpr/ppermute | solution.py:13
  276.5 6.2 %collective-permute-start.1 = (f32[1,16,1024]{2,1,0:T(8,128)S(1)}, f32[1,16,1024]{2,1,0:T(8,128)S(1)}, u32[]{:S(2)}, u32[]{:S(2)}) collective-permute-start(f32[1,16,1024]{2,1,0:T(8,128)S(1)} %get-tuple-element.353), channel_id=1, source_target_pairs={{8,0},{16,8},{24,16},{32,24},{40,32},{48,40},{56,48},{64,56},{72,6... | collective-permute-start | bytes 196616 | tf_op jit(solution)/shard_map/while/body/eval_jaxpr/ppermute | solution.py:13
  283.2 5.2 %collective-permute-start = (f32[1,16,1024]{2,1,0:T(8,128)S(1)}, f32[1,16,1024]{2,1,0:T(8,128)S(1)}, u32[]{:S(2)}, u32[]{:S(2)}) collective-permute-start(f32[1,16,1024]{2,1,0:T(8,128)S(1)} %get-tuple-element.352), channel_id=1, source_target_pairs={{0,8},{8,16},{16,24},{24,32},{32,40},{40,48},{48,56},{56,64},{64,7... | collective-permute-start | bytes 196616 | tf_op jit(solution)/shard_map/while/body/eval_jaxpr/ppermute | solution.py:13
  286.5 6.2 %collective-permute-start.1 = (f32[1,16,1024]{2,1,0:T(8,128)S(1)}, f32[1,16,1024]{2,1,0:T(8,128)S(1)}, u32[]{:S(2)}, u32[]{:S(2)}) collective-permute-start(f32[1,16,1024]{2,1,0:T(8,128)S(1)} %get-tuple-element.353), channel_id=1, source_target_pairs={{8,0},{16,8},{24,16},{32,24},{40,32},{48,40},{56,48},{64,56},{72,6... | collective-permute-start | bytes 196616 | tf_op jit(solution)/shard_map/while/body/eval_jaxpr/ppermute | solution.py:13
  293.1 5.0 %collective-permute-start = (f32[1,16,1024]{2,1,0:T(8,128)S(1)}, f32[1,16,1024]{2,1,0:T(8,128)S(1)}, u32[]{:S(2)}, u32[]{:S(2)}) collective-permute-start(f32[1,16,1024]{2,1,0:T(8,128)S(1)} %get-tuple-element.352), channel_id=1, source_target_pairs={{0,8},{8,16},{16,24},{24,32},{32,40},{40,48},{48,56},{56,64},{64,7... | collective-permute-start | bytes 196616 | tf_op jit(solution)/shard_map/while/body/eval_jaxpr/ppermute | solution.py:13
  296.3 6.2 %collective-permute-start.1 = (f32[1,16,1024]{2,1,0:T(8,128)S(1)}, f32[1,16,1024]{2,1,0:T(8,128)S(1)}, u32[]{:S(2)}, u32[]{:S(2)}) collective-permute-start(f32[1,16,1024]{2,1,0:T(8,128)S(1)} %get-tuple-element.353), channel_id=1, source_target_pairs={{8,0},{16,8},{24,16},{32,24},{40,32},{48,40},{56,48},{64,56},{72,6... | collective-permute-start | bytes 196616 | tf_op jit(solution)/shard_map/while/body/eval_jaxpr/ppermute | solution.py:13
  302.9 5.2 %collective-permute-start = (f32[1,16,1024]{2,1,0:T(8,128)S(1)}, f32[1,16,1024]{2,1,0:T(8,128)S(1)}, u32[]{:S(2)}, u32[]{:S(2)}) collective-permute-start(f32[1,16,1024]{2,1,0:T(8,128)S(1)} %get-tuple-element.352), channel_id=1, source_target_pairs={{0,8},{8,16},{16,24},{24,32},{32,40},{40,48},{48,56},{56,64},{64,7... | collective-permute-start | bytes 196616 | tf_op jit(solution)/shard_map/while/body/eval_jaxpr/ppermute | solution.py:13
  306.3 6.2 %collective-permute-start.1 = (f32[1,16,1024]{2,1,0:T(8,128)S(1)}, f32[1,16,1024]{2,1,0:T(8,128)S(1)}, u32[]{:S(2)}, u32[]{:S(2)}) collective-permute-start(f32[1,16,1024]{2,1,0:T(8,128)S(1)} %get-tuple-element.353), channel_id=1, source_target_pairs={{8,0},{16,8},{24,16},{32,24},{40,32},{48,40},{56,48},{64,56},{72,6... | collective-permute-start | bytes 196616 | tf_op jit(solution)/shard_map/while/body/eval_jaxpr/ppermute | solution.py:13
  312.9 5.3 %collective-permute-start = (f32[1,16,1024]{2,1,0:T(8,128)S(1)}, f32[1,16,1024]{2,1,0:T(8,128)S(1)}, u32[]{:S(2)}, u32[]{:S(2)}) collective-permute-start(f32[1,16,1024]{2,1,0:T(8,128)S(1)} %get-tuple-element.352), channel_id=1, source_target_pairs={{0,8},{8,16},{16,24},{24,32},{32,40},{40,48},{48,56},{56,64},{64,7... | collective-permute-start | bytes 196616 | tf_op jit(solution)/shard_map/while/body/eval_jaxpr/ppermute | solution.py:13
  316.4 6.5 %collective-permute-start.1 = (f32[1,16,1024]{2,1,0:T(8,128)S(1)}, f32[1,16,1024]{2,1,0:T(8,128)S(1)}, u32[]{:S(2)}, u32[]{:S(2)}) collective-permute-start(f32[1,16,1024]{2,1,0:T(8,128)S(1)} %get-tuple-element.353), channel_id=1, source_target_pairs={{8,0},{16,8},{24,16},{32,24},{40,32},{48,40},{56,48},{64,56},{72,6... | collective-permute-start | bytes 196616 | tf_op jit(solution)/shard_map/while/body/eval_jaxpr/ppermute | solution.py:13
  323.4 5.3 %collective-permute-start = (f32[1,16,1024]{2,1,0:T(8,128)S(1)}, f32[1,16,1024]{2,1,0:T(8,128)S(1)}, u32[]{:S(2)}, u32[]{:S(2)}) collective-permute-start(f32[1,16,1024]{2,1,0:T(8,128)S(1)} %get-tuple-element.352), channel_id=1, source_target_pairs={{0,8},{8,16},{16,24},{24,32},{32,40},{40,48},{48,56},{56,64},{64,7... | collective-permute-start | bytes 196616 | tf_op jit(solution)/shard_map/while/body/eval_jaxpr/ppermute | solution.py:13
  326.8 6.2 %collective-permute-start.1 = (f32[1,16,1024]{2,1,0:T(8,128)S(1)}, f32[1,16,1024]{2,1,0:T(8,128)S(1)}, u32[]{:S(2)}, u32[]{:S(2)}) collective-permute-start(f32[1,16,1024]{2,1,0:T(8,128)S(1)} %get-tuple-element.353), channel_id=1, source_target_pairs={{8,0},{16,8},{24,16},{32,24},{40,32},{48,40},{56,48},{64,56},{72,6... | collective-permute-start | bytes 196616 | tf_op jit(solution)/shard_map/while/body/eval_jaxpr/ppermute | solution.py:13
  333.5 4.7 %collective-permute-start = (f32[1,16,1024]{2,1,0:T(8,128)S(1)}, f32[1,16,1024]{2,1,0:T(8,128)S(1)}, u32[]{:S(2)}, u32[]{:S(2)}) collective-permute-start(f32[1,16,1024]{2,1,0:T(8,128)S(1)} %get-tuple-element.352), channel_id=1, source_target_pairs={{0,8},{8,16},{16,24},{24,32},{32,40},{40,48},{48,56},{56,64},{64,7... | collective-permute-start | bytes 196616 | tf_op jit(solution)/shard_map/while/body/eval_jaxpr/ppermute | solution.py:13
  336.2 6.2 %collective-permute-start.1 = (f32[1,16,1024]{2,1,0:T(8,128)S(1)}, f32[1,16,1024]{2,1,0:T(8,128)S(1)}, u32[]{:S(2)}, u32[]{:S(2)}) collective-permute-start(f32[1,16,1024]{2,1,0:T(8,128)S(1)} %get-tuple-element.353), channel_id=1, source_target_pairs={{8,0},{16,8},{24,16},{32,24},{40,32},{48,40},{56,48},{64,56},{72,6... | collective-permute-start | bytes 196616 | tf_op jit(solution)/shard_map/while/body/eval_jaxpr/ppermute | solution.py:13
  (4 other events, 3.2 us)
